TPU v7x, 256 devices: a whole 4x4x8 slice. The times are simulated.
256 devices in a mesh: blk: 8 (over y, core), req: 32 (over z, x).
Axes of the slice: x: 4, y: 4, z: 8, core: 2. Of those that a mesh axis runs over, the one named last changes fastest.
Arguments:
- hidden: bfloat16 [12288, 8192], P('req', 'blk'), may hold values from -120 to 120
- input_norm_gain: float32 [8192], replicated, may hold values from 0.1 to 1.9
- query_weight: bfloat16 [8192, 8192], P('req', 'blk')
- keyvalue_weight: bfloat16 [8192, 2048], P('req', 'blk')
- adapter_down: bfloat16 [32, 3, 16, 8192], P('req', None, None, 'blk'), may hold values from -0.0625 to 0.0625
- adapter_up_query: bfloat16 [32, 16, 8192], P('req', None, 'blk'), may hold values from -1.5 to 1.5
- adapter_up_keyvalue: bfloat16 [32, 16, 2048], P('req', None, 'blk'), may hold values from -1.5 to 1.5
- packed_lengths: int32 [32, 4], P('req'), may hold values from 1 to 192, 384 in all within a row
- prompt_adapter: int32 [32, 4], P('req'), may hold values from 0 to 31
Outputs:
- context: bfloat16 [12288, 8192], P('req', 'blk')
- key_cache: bfloat16 [12288, 1024], P('req', 'blk')
- value_cache: bfloat16 [12288, 1024], P('req', 'blk')
Inputs may be any that keep to these rules, and one draw needn't show every extreme that they name: `packed_lengths`: each row sums to 384; the longest prompt of the whole draw has 192 tokens.
All inputs are finite; a program needn't handle non-finite values.
Results may differ from a plain program's by a relative error of at most 0.012.
The roundings to bfloat16 on the way count: a program that leaves them out, or rounds other values in their place, can miss the bound.
Values may be sent and summed in bfloat16 or wider, within the bound.
A program may use at most 128 MiB of HBM per device.

v0:
```python
import math
import jax
import jax.numpy as jnp
from jax import lax
from jax.sharding import PartitionSpec as P

HEAD_WIDTH = 128
QUERY_LOCAL = 8
KEYVALUE_LOCAL = 1
epsilon = 1e-05
adapter_scale = 2.0
rope_base = 10000.0


def apply_rotation(vectors, cosine_table, sine_table):
    half_size = vectors.shape[-1] // 2
    first_half = vectors[..., :half_size]
    second_half = vectors[..., half_size:]
    turned = jnp.concatenate([-second_half, first_half], axis=-1)
    return vectors * cosine_table + turned * sine_table


def layout(lengths, count):
    slot_index = jnp.arange(count, dtype=jnp.int32)
    prompt_ends = jnp.cumsum(lengths)
    prompt_starts = prompt_ends - lengths
    member = (slot_index[:, None] >= prompt_starts[None, :]) & (
        slot_index[:, None] < prompt_ends[None, :]
    )
    position = jnp.sum(jnp.where(member, slot_index[:, None] - prompt_starts[None, :], 0), axis=1)
    owner = jnp.sum((slot_index[:, None] >= prompt_ends[None, :]).astype(jnp.int32), axis=1)
    return (member.astype(jnp.float32), position, owner, slot_index)


def rope_tables(position, head_size):
    frequency = rope_base ** (-(jnp.arange(head_size // 2, dtype=jnp.float32) * 2.0 / head_size))
    angles = position.astype(jnp.float32)[:, None] * frequency[None, :]
    cosine_table = jnp.cos(angles)
    sine_table = jnp.sin(angles)
    return (
        jnp.concatenate([cosine_table, cosine_table], 1)[:, None, :],
        jnp.concatenate([sine_table, sine_table], 1)[:, None, :],
    )


def shards(
    hidden,
    input_norm_gain,
    query_weight,
    keyvalue_weight,
    adapter_down,
    adapter_up_query,
    adapter_up_keyvalue,
    packed_lengths,
    prompt_adapter,
):
    row_number, feature_cols = hidden.shape
    full_width = feature_cols * lax.axis_size("blk")
    offset = lax.axis_index("blk") * feature_cols
    values = hidden.astype(jnp.float32)
    gain_part = lax.dynamic_slice_in_dim(input_norm_gain, offset, feature_cols, 0)
    squares = lax.psum(jnp.sum(values * values, axis=1), "blk")
    factor = lax.rsqrt(squares / full_width + epsilon)
    normed_part = (values * factor[:, None] * gain_part[None, :]).astype(jnp.bfloat16)
    normed = lax.all_gather(normed_part, "blk", axis=1, tiled=True)
    query_cols = query_weight.shape[1]

    def add_rows(weight_piece):
        return jnp.dot(normed, weight_piece, preferred_element_type=jnp.float32)

    query_plain = add_rows(lax.all_gather(query_weight, "req", axis=0, tiled=True))
    base_pair = add_rows(lax.all_gather(keyvalue_weight, "req", axis=0, tiled=True))
    down_all, up_query_all, up_pair_all = (
        lax.all_gather(adapter_down, "req", axis=0, tiled=True),
        lax.all_gather(adapter_up_query, "req", axis=0, tiled=True),
        lax.all_gather(adapter_up_keyvalue, "req", axis=0, tiled=True),
    )
    adapter_count = down_all.shape[0]
    lengths = packed_lengths[0]
    member, position, owner, slot_index = layout(lengths, row_number)
    prompt_count = lengths.shape[0]
    picked_adapter = (
        prompt_adapter[0][:, None] == jnp.arange(adapter_count, dtype=jnp.int32)[None, :]
    ).astype(jnp.bfloat16)
    down_selected = jnp.einsum(
        "pa,ajrd->pjrd", picked_adapter, down_all, preferred_element_type=jnp.float32
    ).astype(jnp.bfloat16)
    rank_size = down_selected.shape[2]
    partial_value = lax.dot_general(
        normed_part,
        down_selected.reshape(prompt_count * 3 * rank_size, feature_cols),
        (((1,), (1,)), ((), ())),
        preferred_element_type=jnp.float32,
    )
    partial_value = partial_value.reshape(row_number, prompt_count, 3, rank_size)
    masked = jnp.sum(partial_value * member[:, :, None, None], axis=1).reshape(
        row_number, 3 * rank_size
    )
    low_rank = lax.psum(masked, "blk").reshape(row_number, 3, rank_size).astype(jnp.bfloat16)
    low_float = low_rank.astype(jnp.float32)

    def spread(column):
        return (
            (member[:, :, None] * low_float[:, None, column, :])
            .astype(jnp.bfloat16)
            .reshape(row_number, prompt_count * rank_size)
        )

    up_query_selected = jnp.einsum(
        "pa,arc->prc", picked_adapter, up_query_all, preferred_element_type=jnp.float32
    ).astype(jnp.bfloat16)
    up_keyvalue_selected = jnp.einsum(
        "pa,arc->prc", picked_adapter, up_pair_all, preferred_element_type=jnp.float32
    ).astype(jnp.bfloat16)
    up_keyvalue_selected = up_keyvalue_selected.reshape(
        prompt_count, rank_size, KEYVALUE_LOCAL, 2, HEAD_WIDTH
    )
    query_update = jnp.dot(
        spread(0),
        up_query_selected.reshape(prompt_count * rank_size, query_cols),
        preferred_element_type=jnp.float32,
    )
    key_update = jnp.dot(
        spread(1),
        up_keyvalue_selected[:, :, :, 0].reshape(
            prompt_count * rank_size, KEYVALUE_LOCAL * HEAD_WIDTH
        ),
        preferred_element_type=jnp.float32,
    )
    value_update = jnp.dot(
        spread(2),
        up_keyvalue_selected[:, :, :, 1].reshape(
            prompt_count * rank_size, KEYVALUE_LOCAL * HEAD_WIDTH
        ),
        preferred_element_type=jnp.float32,
    )
    cosine_table, sine_table = rope_tables(position, HEAD_WIDTH)
    query_complete = (query_plain + adapter_scale * query_update).reshape(
        row_number, QUERY_LOCAL * KEYVALUE_LOCAL, HEAD_WIDTH
    )
    query_states = apply_rotation(query_complete, cosine_table, sine_table).astype(jnp.bfloat16)
    keyvalue_plain = base_pair.reshape(row_number, KEYVALUE_LOCAL, 2, HEAD_WIDTH)
    key_vectors = apply_rotation(
        keyvalue_plain[:, :, 0]
        + adapter_scale * key_update.reshape(row_number, KEYVALUE_LOCAL, HEAD_WIDTH),
        cosine_table,
        sine_table,
    ).astype(jnp.bfloat16)
    value_vectors = (
        keyvalue_plain[:, :, 1]
        + adapter_scale * value_update.reshape(row_number, KEYVALUE_LOCAL, HEAD_WIDTH)
    ).astype(jnp.bfloat16)
    grouped = query_states.reshape(row_number, KEYVALUE_LOCAL, QUERY_LOCAL, HEAD_WIDTH)
    scores = jnp.einsum(
        "tkgc,skc->kgts", grouped, key_vectors, preferred_element_type=jnp.float32
    ) / math.sqrt(HEAD_WIDTH)
    allowed = (owner[:, None] == owner[None, :]) & (slot_index[None, :] <= slot_index[:, None])
    scores = jnp.where(allowed[None, None], scores, -1e30)
    row_max = jnp.max(scores, axis=-1, keepdims=True)
    exponent = jnp.exp(scores - row_max)
    attend = (exponent / jnp.sum(exponent, axis=-1, keepdims=True)).astype(jnp.bfloat16)
    context = jnp.einsum(
        "kgts,skc->tkgc", attend, value_vectors, preferred_element_type=jnp.float32
    ).astype(jnp.bfloat16)
    return (
        context.reshape(row_number, KEYVALUE_LOCAL * QUERY_LOCAL * HEAD_WIDTH),
        key_vectors.reshape(row_number, KEYVALUE_LOCAL * HEAD_WIDTH),
        value_vectors.reshape(row_number, KEYVALUE_LOCAL * HEAD_WIDTH),
    )


def solution(mesh):
    in_specs = (
        P("req", "blk"),
        P(),
        P("req", "blk"),
        P("req", "blk"),
        P("req", None, None, "blk"),
        P("req", None, "blk"),
        P("req", None, "blk"),
        P("req", None),
        P("req", None),
    )
    out_specs = (P("req", "blk"), P("req", "blk"), P("req", "blk"))
    return jax.shard_map(shards, mesh=mesh, in_specs=in_specs, out_specs=out_specs, check_vma=False)
```

profile of v0, /device:TPU:1, one launch (start us, length us, event | category | flops | bytes accessed | tf_op | source)
XLA Modules:
  0.0 463.0 jit_solution(1548275453089813098)
XLA Ops:
  7.2 0.7 all-gather.14.cloned.1.call-update
  8.0 0.7 all-gather.10.cloned.1.call-update
  8.7 0.7 all-gather.8.cloned.1.call-update
  9.4 0.7 dynamic_slice.3
  10.1 1.4 fusion.7
  11.5 15.0 %psum.14 = f32[384]{0:T(512)S(1)} all-reduce(f32[384]{0:T(512)S(1)} %fusion.7), channel_id=1, replica_groups=mesh['blk'=8,'req'=32] {'blk'}, use_global_device_ids=true, to_apply=%region_1.0 | all-reduce | flops 384 | bytes 3072 | tf_op jit(solution)/shard_map/psum | solution.py:62
  26.6 1.1 fusion.9
  28.5 40.4 %all_gather.21 = bf16[32,16,256]{2,1,0:T(8,128)(2,1)S(1)} all-gather(bf16[1,16,256]{2,1,0:T(8,128)(2,1)S(1)} %copy-done.4), channel_id=1, replica_groups=mesh['blk'=8,'req'=32] {'req'}, dimensions={0}, use_global_device_ids=true | all-gather | bytes 270336 | tf_op jit(solution)/shard_map/all_gather | solution.py:76
  69.6 0.8 multiply_cosine_fusion
  70.4 16.0 %all-gather.14.cloned.1.call-done = bf16[32,16,1024]{2,1,0:T(8,128)(2,1)} async-done(((bf16[1,16,1024]{2,1,0:T(8,128)(2,1)}), bf16[32,16,1024]{2,1,0:T(8,128)(2,1)}) %all-gather.14.cloned.1.call-update) | async-done | bytes 1048592 | tf_op jit(solution)/shard_map/all_gather | solution.py:75
  86.3 2.4 convolution_convert_fusion
  88.8 78.0 %all-gather.10.cloned.1.call-done = bf16[32,3,16,1024]{3,2,1,0:T(8,128)(2,1)} async-done(((bf16[1,3,16,1024]{3,2,1,0:T(8,128)(2,1)}), bf16[32,3,16,1024]{3,2,1,0:T(8,128)(2,1)}) %all-gather.10.cloned.1.call-update) | async-done | bytes 3145744 | tf_op jit(solution)/shard_map/all_gather | solution.py:74
  166.8 5.4 %fusion.15 = bf16[4,3,16,1024]{3,0,2,1:T(4,128)(2,1)S(1)} fusion(bf16[32,3,16,1024]{3,2,1,0:T(8,128)(2,1)} %all-gather.10.cloned.1.call-done, s32[4]{0:T(128)S(1)} %bitcast.137), kind=kOutput, calls=%fused_computation.23 | convolution fusion | flops 12779648 | bytes 3538960 | tf_op jit(solution)/shard_map/pa,ajrd->pjrd/dot_general | solution.py:85
  172.6 26.5 %psum.15 = bf16[384,48]{0,1:T(8,128)(2,1)S(1)} all-reduce(f32[384,48]{0,1:T(8,128)S(1)} %bitcast.132), channel_id=1, replica_groups=mesh['blk'=8,'req'=32] {'blk'}, use_global_device_ids=true, to_apply=%region_4.5 | all-reduce | flops 18432 | bytes 110592 | tf_op jit(solution)/shard_map/psum | solution.py:99
  199.5 49.6 %all-gather.8.cloned.1.call-done = bf16[8192,256]{1,0:T(8,128)(2,1)} async-done(((bf16[256,256]{1,0:T(8,128)(2,1)}), bf16[8192,256]{1,0:T(8,128)(2,1)}) %all-gather.8.cloned.1.call-update) | async-done | bytes 4194320 | tf_op jit(solution)/shard_map/all_gather | solution.py:72
  249.1 46.2 %all-gather.6.cloned.1.call-done = bf16[384,8192]{1,0:T(8,128)(2,1)} async-done(((bf16[384,1024]{1,0:T(8,128)(2,1)}), bf16[384,8192]{1,0:T(8,128)(2,1)}) %all-gather.6.cloned.1.call-update) | async-done | bytes 6291472 | tf_op jit(solution)/shard_map/all_gather | solution.py:65
  295.4 6.4 %fusion.55 = f32[384,256]{0,1:T(8,128)S(1)} fusion(bf16[384,8192]{1,0:T(8,128)(2,1)} %all-gather.6.cloned.1.call-done, bf16[8192,256]{1,0:T(8,128)(2,1)} %all-gather.8.cloned.1.call-done), kind=kOutput, calls=%fused_computation.86 | convolution fusion | flops 1610612736 | bytes 10878976 | tf_op jit(solution)/shard_map/dot_general | solution.py:69
  302.9 134.8 %all-gather.12.cloned.1.call-done = bf16[8192,1024]{1,0:T(8,128)(2,1)} async-done(((bf16[256,1024]{1,0:T(8,128)(2,1)}), bf16[8192,1024]{1,0:T(8,128)(2,1)}) %all-gather.12.cloned.1.call-update) | async-done | bytes 16777232 | tf_op jit(solution)/shard_map/all_gather | solution.py:71
  437.7 12.0 %fusion.11 = f32[384,1024]{1,0:T(8,128)S(1)} fusion(f32[384,1024,1]{1,0,2:T(8,128)S(1)} %fusion.34, bf16[384,8192]{1,0:T(8,128)(2,1)} %all-gather.6.cloned.1.call-done, bf16[8192,1024]{1,0:T(8,128)(2,1)} %all-gather.12.cloned.1.call-done), kind=kOutput, calls=%fused_computation.21 | convolution fusion | flops 6443237376 | bytes 26214400 | tf_op jit(solution)/shard_map/dot_general | solution.py:69
  450.6 0.6 maximum_multiply_fusion
  451.2 1.4 fusion.1
  452.7 1.0 fusion
  453.7 1.6 fusion.12
  455.3 1.2 copy.43
  (49 shorter events, 4.5 us)
Async XLA Ops:
  7.2 19.4 %copy-start = (bf16[384,1024]{1,0:T(8,128)(2,1)S(1)}, bf16[384,1024]{1,0:T(8,128)(2,1)}, u32[]{:S(2)}) copy-start(bf16[384,1024]{1,0:T(8,128)(2,1)} %param.9) | copy-start | bytes 2359300
  7.2 79.1 %all-gather.14.cloned.1.call-start = ((), (), s32[]{:S(2)}) async-start(), calls=%async_computation.4 | async-start | bytes 1081344 | tf_op jit(solution)/shard_map/all_gather | solution.py:75
  7.9 158.9 %all-gather.10.cloned.1.call-start = ((), (), s32[]{:S(2)}) async-start(), calls=%async_computation.2 | async-start | bytes 3244032 | tf_op jit(solution)/shard_map/all_gather | solution.py:74
  8.7 240.5 %all-gather.8.cloned.1.call-start = ((), (), s32[]{:S(2)}) async-start(), calls=%async_computation.1 | async-start | bytes 4325376 | tf_op jit(solution)/shard_map/all_gather | solution.py:72
  9.4 286.0 %all-gather.6.cloned.1.call-start = ((), (), s32[]{:S(2)}) async-start(), calls=%async_computation | async-start | bytes 7077888 | tf_op jit(solution)/shard_map/all_gather | solution.py:65
  11.5 16.8 %copy-start.6 = (s32[1,4]{1,0:T(1,128)S(1)}, s32[1,4]{1,0:T(1,128)}, u32[]{:S(2)}) copy-start(s32[1,4]{1,0:T(1,128)} %param.16) | copy-start | bytes 52
  11.5 17.0 %copy-start.4 = (bf16[1,16,256]{2,1,0:T(8,128)(2,1)S(1)}, bf16[1,16,256]{2,1,0:T(8,128)(2,1)}, u32[]{:S(2)}) copy-start(bf16[1,16,256]{2,1,0:T(8,128)(2,1)} %param.15) | copy-start | bytes 24580
  26.5 42.4 %copy-start.5 = (s32[1,4]{1,0:T(1,128)S(1)}, s32[1,4]{1,0:T(1,128)}, u32[]{:S(2)}) copy-start(s32[1,4]{1,0:T(1,128)} %param.17) | copy-start | bytes 52
  27.7 410.0 %all-gather.12.cloned.1.call-start = ((), (), s32[]{:S(2)}) async-start(), calls=%async_computation.3 | async-start | bytes 17301504 | tf_op jit(solution)/shard_map/all_gather | solution.py:71
  88.8 83.4 %copy-start.1 = (bf16[384,1024]{1,0:T(8,128)(2,1)S(1)}, bf16[384,1024]{1,0:T(8,128)(2,1)}, u32[]{:S(2)}) copy-start(bf16[384,1024]{1,0:T(8,128)(2,1)} %fusion.9) | copy-start | bytes 2359300
  302.3 151.4 %copy-start.3 = (bf16[384,128]{1,0:T(8,128)(2,1)}, bf16[384,128]{1,0:T(8,128)(2,1)S(1)}, u32[]{:S(2)}) copy-start(bf16[384,128]{1,0:T(8,128)(2,1)S(1)} %fusion.21) | copy-start | bytes 294916
  302.9 148.4 %copy-start.2 = (bf16[384,128]{1,0:T(8,128)(2,1)}, bf16[384,128]{1,0:T(8,128)(2,1)S(1)}, u32[]{:S(2)}) copy-start(bf16[384,128]{1,0:T(8,128)(2,1)S(1)} %get-tuple-element.18) | copy-start | bytes 294916
Sparse Core Ops, SparseCore 0:
  10.6 75.6 all-gather.13
  88.9 77.8 all-gather.9
  169.3 79.7 all-gather.7
  251.4 43.9 all-gather.5
  297.8 139.8 all-gather.11
where the time goes:
time: 463 us
  waiting for transfers between devices  327 us (71%)
  blocking collectives  81.9 us (18%)
  matrix products  30.7 us (7%)
  between operations  14 us (3%)
  other arithmetic  6.18 us (1%)
    all_gather x1, waiting for transfers between devices, shards(): lax.all_gather(query_weight, 'req', axis=0, tiled=True)  135 us
    all_gather x1, waiting for transfers between devices, shards(): lax.all_gather(adapter_down, 'req', axis=0, tiled=True)  78 us
    all_gather x1, waiting for transfers between devices, shards(): lax.all_gather(keyvalue_weight, 'req', axis=0, tiled=True)  49.6 us
    all_gather x1, waiting for transfers between devices, shards(): normed = lax.all_gather(normed_part, 'blk', axis=1, tiled=True)  46.2 us
    all_gather x1, blocking collectives, shards(): lax.all_gather(adapter_up_keyvalue, 'req', axis=0, tiled=True)  40.4 us
    psum x1, blocking collectives, shards(): lax.psum(masked, 'blk').reshape(row_number, 3, rank_size)  26.5 us
    dot_general x2, matrix products, add_rows(): return jnp.dot(normed, weight_piece, preferred_element_type=jnp.float32)  18.4 us
    all_gather x1, waiting for transfers between devices, shards(): lax.all_gather(adapter_up_query, 'req', axis=0, tiled=True)  16 us
  transfers between devices with their start and end apart: 5, of which 5 were waited for; matrix products, arithmetic and copies ran while one was open for 5% of the time, Pallas kernels for 0%

commit v1 on v0

--- a/solution.py
+++ b/solution.py
@@ -71,7 +71,9 @@
     query_plain = add_rows(lax.all_gather(query_weight, "req", axis=0, tiled=True))
     base_pair = add_rows(lax.all_gather(keyvalue_weight, "req", axis=0, tiled=True))
     down_all, up_query_all, up_pair_all = (
-        lax.all_gather(adapter_down, "req", axis=0, tiled=True),
+        jnp.concatenate(
+            lax.all_to_all(jnp.stack([adapter_down] * lax.axis_size("req")), "req", 0, 0), axis=0
+        ),
         lax.all_gather(adapter_up_query, "req", axis=0, tiled=True),
         lax.all_gather(adapter_up_keyvalue, "req", axis=0, tiled=True),
     )

time: 463 us -> 412 us (0.89)
  waiting for transfers between devices: 327 us -> 188 us
  blocking collectives: 81.9 us -> 156 us
  starting transfers between devices: 0.19 us -> 9.76 us
    all_gather x1 -> x0, waiting for transfers between devices: 78 us -> none  [shards(): lax.all_gather(adapter_down, 'req', axis=0, tiled=True)]
    all_gather x1, blocking collectives: 40.4 us -> 105 us  [shards(): lax.all_gather(adapter_up_keyvalue, 'req', axis=0, tiled=True)]
    all_gather x1, waiting for transfers between devices: 49.6 us -> 5.45 us  [shards(): lax.all_gather(keyvalue_weight, 'req', axis=0, tiled=True)]
    all_gather x1, waiting for transfers between devices: 16 us -> 0.01 us  [shards(): lax.all_gather(adapter_up_query, 'req', axis=0, tiled=True)]
    all_to_all x0 -> x1, starting transfers between devices: none -> 9.61 us  [shards(): lax.all_to_all(jnp.stack([adapter_down] * lax.axis_size('req')), 'req', 0...]
    psum x1, blocking collectives: 26.5 us -> 35.5 us  [shards(): lax.psum(masked, 'blk').reshape(row_number, 3, rank_size)]
  transfers between devices with their start and end apart: 5 -> 5, of which waited for: 5 -> 3; matrix products, arithmetic and copies ran while one was open for 5% -> 6% of each run, Pallas kernels for 0% -> 0%
where the time goes in v1:
time: 412 us; the launch traced here: 411 us
  waiting for transfers between devices  188 us (46%)
  blocking collectives  156 us (38%)
  matrix products  30.4 us (7%)
  between operations  14 us (3%)
  starting transfers between devices  9.76 us (2%)
  other arithmetic  8 us (2%)
  local copies, waits for them, and re-layouts  4.89 us (1%)
    all_gather x1, waiting for transfers between devices, shards(): lax.all_gather(query_weight, 'req', axis=0, tiled=True)  135 us
    all_gather x1, blocking collectives, shards(): lax.all_gather(adapter_up_keyvalue, 'req', axis=0, tiled=True)  105 us
    all_gather x1, waiting for transfers between devices, shards(): normed = lax.all_gather(normed_part, 'blk', axis=1, tiled=True)  46.2 us
    psum x1, blocking collectives, shards(): lax.psum(masked, 'blk').reshape(row_number, 3, rank_size)  35.5 us
    dot_general x2, matrix products, add_rows(): return jnp.dot(normed, weight_piece, preferred_element_type=jnp.float32)  18.4 us
    psum x1, blocking collectives, shards(): squares = lax.psum(jnp.sum(values * values, axis=1), 'blk')  15 us
    all_to_all x1, starting transfers between devices, shards(): lax.all_to_all(jnp.stack([adapter_down] * lax.axis_size('req')), 'req', 0...  9.61 us
  transfers between devices with their start and end apart: 5, of which 3 were waited for; matrix products, arithmetic and copies ran while one was open for 6% of the time, Pallas kernels for 0%

profile of v1, /device:TPU:1, one launch (start us, length us, event | category | flops | bytes accessed | tf_op | source)
XLA Modules:
  0.0 411.2 jit_solution(17709250622139892717)
XLA Ops:
  7.2 0.7 all-gather.11.cloned.1.call-update
  8.0 0.7 all-gather.7.cloned.1.call-update
  8.7 0.7 dynamic_slice.3
  9.4 1.4 fusion.8
  10.8 15.0 %psum.14 = f32[384]{0:T(512)S(1)} all-reduce(f32[384]{0:T(512)S(1)} %fusion.8), channel_id=1, replica_groups=mesh['blk'=8,'req'=32] {'blk'}, use_global_device_ids=true, to_apply=%region_1.0 | all-reduce | flops 384 | bytes 3072 | tf_op jit(solution)/shard_map/psum | solution.py:62
  25.8 2.3 fusion.10
  28.7 2.1 stack.2
  30.8 9.6 %all-to-all-start = ((bf16[32,1,3,16,1024]{4,3,2,1,0:T(8,128)(2,1)}), bf16[32,1,3,16,1024]{4,3,2,1,0:T(8,128)(2,1)S(1)}, u32[]{:S(2)}, u32[]{:S(2)}) async-start(bf16[32,1,3,16,1024]{4,3,2,1,0:T(8,128)(2,1)} %stack.2), calls=%async_computation | async-start | bytes 6291456 | tf_op jit(solution)/shard_map/all_to_all | solution.py:75
  40.6 105.3 %all_gather.17 = bf16[32,16,256]{2,1,0:T(8,128)(2,1)S(1)} all-gather(bf16[1,16,256]{2,1,0:T(8,128)(2,1)S(1)} %copy-done.5), channel_id=1, replica_groups=mesh['blk'=8,'req'=32] {'req'}, dimensions={0}, use_global_device_ids=true | all-gather | bytes 270336 | tf_op jit(solution)/shard_map/all_gather | solution.py:78
  146.6 1.4 multiply_cosine_fusion
  148.0 3.1 convolution_convert_fusion
  151.1 3.5 fusion.16
  155.1 35.5 %psum.15 = bf16[384,48]{0,1:T(8,128)(2,1)S(1)} all-reduce(f32[384,48]{0,1:T(8,128)S(1)} %bitcast.139), channel_id=1, replica_groups=mesh['blk'=8,'req'=32] {'blk'}, use_global_device_ids=true, to_apply=%region_4.5 | all-reduce | flops 18432 | bytes 110592 | tf_op jit(solution)/shard_map/psum | solution.py:101
  190.6 1.3 fusion.35
  191.9 5.4 %all-gather.7.cloned.1.call-done = bf16[8192,256]{1,0:T(8,128)(2,1)} async-done(((bf16[256,256]{1,0:T(8,128)(2,1)}), bf16[8192,256]{1,0:T(8,128)(2,1)}) %all-gather.7.cloned.1.call-update) | async-done | bytes 4194320 | tf_op jit(solution)/shard_map/all_gather | solution.py:72
  197.4 46.2 %all-gather.5.cloned.1.call-done = bf16[384,8192]{1,0:T(8,128)(2,1)} async-done(((bf16[384,1024]{1,0:T(8,128)(2,1)}), bf16[384,8192]{1,0:T(8,128)(2,1)}) %all-gather.5.cloned.1.call-update) | async-done | bytes 6291472 | tf_op jit(solution)/shard_map/all_gather | solution.py:65
  243.5 6.4 %fusion.56 = f32[384,256]{0,1:T(8,128)S(1)} fusion(bf16[384,8192]{1,0:T(8,128)(2,1)} %all-gather.5.cloned.1.call-done, bf16[8192,256]{1,0:T(8,128)(2,1)} %all-gather.7.cloned.1.call-done), kind=kOutput, calls=%fused_computation.87 | convolution fusion | flops 1610612736 | bytes 10878976 | tf_op jit(solution)/shard_map/dot_general | solution.py:69
  251.1 134.8 %all-gather.9.cloned.1.call-done = bf16[8192,1024]{1,0:T(8,128)(2,1)} async-done(((bf16[256,1024]{1,0:T(8,128)(2,1)}), bf16[8192,1024]{1,0:T(8,128)(2,1)}) %all-gather.9.cloned.1.call-update) | async-done | bytes 16777232 | tf_op jit(solution)/shard_map/all_gather | solution.py:71
  385.8 12.0 %fusion.12 = f32[384,1024]{1,0:T(8,128)S(1)} fusion(f32[384,1024,1]{1,0,2:T(8,128)S(1)} %fusion.35, bf16[384,8192]{1,0:T(8,128)(2,1)} %all-gather.5.cloned.1.call-done, bf16[8192,1024]{1,0:T(8,128)(2,1)} %all-gather.9.cloned.1.call-done), kind=kOutput, calls=%fused_computation.22 | convolution fusion | flops 6443237376 | bytes 26214400 | tf_op jit(solution)/shard_map/dot_general | solution.py:69
  398.7 0.6 maximum_multiply_fusion
  399.4 1.4 fusion.1
  400.8 1.0 fusion
  401.9 1.6 fusion.13
  403.5 1.2 copy.56
  (51 shorter events, 4.0 us)
Async XLA Ops:
  7.2 21.5 %copy-start.3 = (bf16[1,3,16,1024]{3,2,1,0:T(8,128)(2,1)S(1)}, bf16[1,3,16,1024]{3,2,1,0:T(8,128)(2,1)}, u32[]{:S(2)}) copy-start(bf16[1,3,16,1024]{3,2,1,0:T(8,128)(2,1)} %param.13) | copy-start | bytes 294916
  7.2 140.9 %all-gather.11.cloned.1.call-start = ((), (), s32[]{:S(2)}) async-start(), calls=%async_computation.4 | async-start | bytes 1081344 | tf_op jit(solution)/shard_map/all_gather | solution.py:77
  7.9 189.5 %all-gather.7.cloned.1.call-start = ((), (), s32[]{:S(2)}) async-start(), calls=%async_computation.2 | async-start | bytes 4325376 | tf_op jit(solution)/shard_map/all_gather | solution.py:72
  8.7 234.9 %all-gather.5.cloned.1.call-start = ((), (), s32[]{:S(2)}) async-start(), calls=%async_computation.1 | async-start | bytes 7077888 | tf_op jit(solution)/shard_map/all_gather | solution.py:65
  28.1 357.8 %all-gather.9.cloned.1.call-start = ((), (), s32[]{:S(2)}) async-start(), calls=%async_computation.3 | async-start | bytes 17301504 | tf_op jit(solution)/shard_map/all_gather | solution.py:71
  30.8 9.6 %copy-start.7 = (s32[1,4]{1,0:T(1,128)S(1)}, s32[1,4]{1,0:T(1,128)}, u32[]{:S(2)}) copy-start(s32[1,4]{1,0:T(1,128)} %param.16) | copy-start | bytes 52
  30.8 9.8 %copy-start.5 = (bf16[1,16,256]{2,1,0:T(8,128)(2,1)S(1)}, bf16[1,16,256]{2,1,0:T(8,128)(2,1)}, u32[]{:S(2)}) copy-start(bf16[1,16,256]{2,1,0:T(8,128)(2,1)} %param.15) | copy-start | bytes 24580
  30.8 115.1 %copy-start.6 = (s32[1,4]{1,0:T(1,128)S(1)}, s32[1,4]{1,0:T(1,128)}, u32[]{:S(2)}) copy-start(s32[1,4]{1,0:T(1,128)} %param.17) | copy-start | bytes 52
  30.8 120.3 %all-to-all-start = ((bf16[32,1,3,16,1024]{4,3,2,1,0:T(8,128)(2,1)}), bf16[32,1,3,16,1024]{4,3,2,1,0:T(8,128)(2,1)S(1)}, u32[]{:S(2)}, u32[]{:S(2)}) async-start(bf16[32,1,3,16,1024]{4,3,2,1,0:T(8,128)(2,1)} %stack.2), calls=%async_computation | async-start | bytes 6291456 | tf_op jit(solution)/shard_map/all_to_all | solution.py:75
  151.1 3.5 copy-start
  249.9 0.9 copy-start.1
  250.5 151.4 %copy-start.4 = (bf16[384,128]{1,0:T(8,128)(2,1)}, bf16[384,128]{1,0:T(8,128)(2,1)S(1)}, u32[]{:S(2)}) copy-start(bf16[384,128]{1,0:T(8,128)(2,1)S(1)} %fusion.22) | copy-start | bytes 294916
  251.1 148.3 %copy-start.2 = (bf16[384,128]{1,0:T(8,128)(2,1)}, bf16[384,128]{1,0:T(8,128)(2,1)S(1)}, u32[]{:S(2)}) copy-start(bf16[384,128]{1,0:T(8,128)(2,1)S(1)} %get-tuple-element.21) | copy-start | bytes 294916
Sparse Core Ops, SparseCore 0:
  10.6 92.9 all-gather.10
  106.1 91.1 all-gather.6
  199.8 43.7 all-gather.4
  246.0 139.8 all-gather.8
